TPU v7x, 512 devices: a whole 4x8x8 slice. The times are simulated.
512 devices in a mesh: dp: 64 (over z, x, y_hi), rep: 8 (over y_lo, core).
Axes of the slice: x: 4, y: 8 (y_hi: 2, y_lo: 4; y = y_hi * 4 + y_lo), z: 8, core: 2. Of those that a mesh axis runs over, the one named last changes fastest.
Arguments:
- tables: bfloat16 [256, 256, 512], P('dp'), may hold values from -130 to 130
- sample_ids: int32 [512, 256, 4], P('rep', 'dp'), may hold values from 0 to 255
- table_slot: int32 [256], replicated, may hold values from 0 to 255, each once
- norm_gain: float32 [512], replicated, may hold values from 0.5 to 1.5
- qkv_weight: bfloat16 [512, 1152], P('dp'), may hold values from -1.1 to 1.1
- out_weight: bfloat16 [512, 384], P('dp'), may hold values from -0.3125 to 0.3125
- cotangent: bfloat16 [512, 256, 512], P(('rep', 'dp')), may hold values from -24 to 24
Outputs:
- layer_out: bfloat16 [512, 256, 512], P(('rep', 'dp'))
- pooled_grad: bfloat16 [512, 256, 512], P('rep', 'dp')
- grad_qkv: float32 [512, 1152], P('dp')
- grad_out: float32 [512, 384], P('dp')
Inputs may be any that keep to these rules, and one draw needn't show every extreme that they name: `table_slot`: each table slot holds the table of exactly one feature.
All inputs are finite; a program needn't handle non-finite values.
Results may differ from a plain program's by a relative error of at most 0.015.
Values may be sent and summed in bfloat16 or wider, within the bound.
A program may use at most 64 MiB of HBM per device.

v0:
```python
import math

import jax
import jax.numpy as jnp
from jax import lax
from jax.sharding import PartitionSpec as P

E = 512
H = 6
DH = 64
F = 256
P_SIZE = 4


norm_eps = 1e-06


def attend(projected, sample_count):
    projected_split = projected.reshape(sample_count, F, 3, H, DH)
    query_part = projected_split[:, :, 0]
    key_part = projected_split[:, :, 1]
    value_part = projected_split[:, :, 2]
    scores = jnp.einsum(
        "sqhd,skhd->shqk", query_part, key_part, preferred_element_type=jnp.float32
    ) * DH ** (-0.5)
    shifted = scores - jnp.max(scores, axis=-1, keepdims=True)
    raised = jnp.exp(shifted)
    soft = (raised / jnp.sum(raised, axis=-1, keepdims=True)).astype(jnp.bfloat16)
    context = jnp.einsum(
        "shqk,skhd->sqhd", soft, value_part, preferred_element_type=jnp.float32
    ).astype(jnp.bfloat16)
    return (context.reshape(sample_count * F, H * DH), soft, query_part, key_part, value_part)


def attend_back(grad_context, soft, query_part, key_part, value_part, sample_count):
    grad_ctx = grad_context.reshape(sample_count, F, H, DH)
    grad_soft = jnp.einsum(
        "sqhd,skhd->shqk", grad_ctx, value_part, preferred_element_type=jnp.float32
    )
    soft_float = soft.astype(jnp.float32)
    inner = jnp.sum(soft_float * grad_soft, axis=-1, keepdims=True)
    grad_scores = (soft_float * (grad_soft - inner) * DH ** (-0.5)).astype(jnp.bfloat16)
    grad_query = jnp.einsum(
        "shqk,skhd->sqhd", grad_scores, key_part, preferred_element_type=jnp.float32
    ).astype(jnp.bfloat16)
    grad_key = jnp.einsum(
        "shqk,sqhd->skhd", grad_scores, query_part, preferred_element_type=jnp.float32
    ).astype(jnp.bfloat16)
    grad_value = jnp.einsum(
        "shqk,sqhd->skhd", soft, grad_ctx, preferred_element_type=jnp.float32
    ).astype(jnp.bfloat16)
    stacked = jnp.stack([grad_query, grad_key, grad_value], axis=2)
    return stacked.reshape(sample_count * F, 3 * H * DH)


def on_device(tables, sample_ids, table_slot, norm_gain, qkv_weight, out_weight, cotangent):
    slot_count = tables.shape[0]
    slot_index = jnp.arange(slot_count, dtype=jnp.int32)[None, :, None]
    gathered = tables[slot_index, sample_ids]
    pooled = (jnp.sum(gathered, axis=2, dtype=jnp.float32) * (1.0 / math.sqrt(P_SIZE))).astype(
        jnp.bfloat16
    )
    arrived = lax.all_to_all(pooled, "dp", split_axis=0, concat_axis=1, tiled=True)
    tokens = jnp.take(arrived, table_slot, axis=1)
    sample_count = tokens.shape[0]
    row_count = sample_count * F
    head_width = H * DH
    token_rows = tokens.reshape(row_count, E)
    cot_rows = cotangent.reshape(row_count, E)
    as_float = token_rows.astype(jnp.float32)
    inverse_rms = lax.rsqrt(jnp.mean(as_float * as_float, axis=-1, keepdims=True) + norm_eps)
    normed = as_float * inverse_rms
    hidden = (normed * norm_gain).astype(jnp.bfloat16)
    full_qkv, full_out = (
        lax.all_gather(qkv_weight, "dp", axis=0, tiled=True),
        lax.all_gather(out_weight, "dp", axis=0, tiled=True),
    )
    projected = jnp.dot(hidden, full_qkv, preferred_element_type=jnp.float32).astype(jnp.bfloat16)
    context, soft, query_part, key_part, value_part = attend(projected, sample_count)
    branch_rows = jnp.dot(context, full_out.T, preferred_element_type=jnp.float32)
    layer_out = (as_float + branch_rows).astype(jnp.bfloat16).reshape(sample_count, F, E)
    grad_context = jnp.dot(cot_rows, full_out, preferred_element_type=jnp.float32).astype(
        jnp.bfloat16
    )
    grad_projected = attend_back(grad_context, soft, query_part, key_part, value_part, sample_count)
    grad_hidden = jnp.dot(grad_projected, full_qkv.T, preferred_element_type=jnp.float32)
    scaled = grad_hidden * norm_gain
    grad_norm = inverse_rms * (scaled - normed * jnp.mean(scaled * normed, axis=-1, keepdims=True))
    grad_tokens = (
        (cot_rows.astype(jnp.float32) + grad_norm).astype(jnp.bfloat16).reshape(sample_count, F, E)
    )
    inverse_slot = jnp.zeros((F,), jnp.int32).at[table_slot].set(jnp.arange(F, dtype=jnp.int32))
    grad_slots = jnp.take(grad_tokens, inverse_slot, axis=1)
    pooled_grad = lax.all_to_all(grad_slots, "dp", split_axis=1, concat_axis=0, tiled=True)
    scale_back = 1.0 / (sample_count * lax.axis_size("dp") * lax.axis_size("rep"))
    owned_rows = lax.psum_scatter(
        jnp.concatenate(
            [
                jnp.dot(hidden.T, grad_projected, preferred_element_type=jnp.float32),
                jnp.dot(cot_rows.T, context, preferred_element_type=jnp.float32),
            ],
            axis=1,
        )
        * scale_back,
        "dp",
        scatter_dimension=0,
        tiled=True,
    )
    grad_rows = lax.psum(owned_rows.astype(jnp.bfloat16), "rep").astype(jnp.float32)
    grad_qkv = grad_rows[:, : 3 * head_width]
    grad_out = grad_rows[:, 3 * head_width :]
    return (layer_out, pooled_grad, grad_qkv, grad_out)


def solution(mesh):
    return jax.shard_map(
        on_device,
        mesh=mesh,
        in_specs=(
            P("dp", None, None),
            P("rep", "dp", None),
            P(),
            P(),
            P("dp", None),
            P("dp", None),
            P(("rep", "dp"), None, None),
        ),
        out_specs=(
            P(("rep", "dp"), None, None),
            P("rep", "dp", None),
            P("dp", None),
            P("dp", None),
        ),
        check_vma=False,
    )
```

profile of v0, /device:TPU:1, one launch (start us, length us, event | category | flops | bytes accessed | tf_op | source)
XLA Modules:
  0.0 1149.3 jit_solution(12226958558484566163)
XLA Ops:
  7.2 0.0 copy-start
  7.2 0.0 all-gather.2.cloned.1.call-start
  7.2 0.7 all-gather.2.cloned.1.call-update
  7.9 0.7 fusion.42
  8.6 0.1 copy.38
  8.8 0.2 reshape.194
  8.9 0.0 copy-done
  8.9 12.3 %gather_fusion = bf16[1024,512]{1,0:T(8,128)(2,1)} fusion(bf16[4,256,512]{2,1,0:T(8,128)(2,1)S(1)} %copy-done, s32[1024]{0:T(1024)S(1)} %reshape.194), kind=kCustom, calls=%fused_computation.2 | custom fusion | bytes 2105344 | tf_op jit(solution)/shard_map/gather | solution.py:59
  21.2 1.7 reshape.211
  22.9 0.0 copy-start.7
  22.9 0.0 copy-start.1
  22.9 2.3 reduce_sum.45
  25.3 1.9 multiply_convert_fusion
  27.1 19.6 %all-to-all-start = ((bf16[64,4,512]{2,1,0:T(4,128)(2,1)}), bf16[64,4,512]{2,1,0:T(4,128)(2,1)S(1)}, u32[]{:S(2)}, u32[]{:S(2)}) async-start(bf16[64,4,512]{2,1,0:T(4,128)(2,1)} %multiply_convert_fusion), calls=%async_computation | async-start | bytes 524288 | tf_op jit(solution)/shard_map/all_to_all | solution.py:63
  46.8 0.0 reduce-scatter.2.cloned.1.call-start
  46.8 0.0 copy-done.7
  46.8 197.9 %all_gather.7 = bf16[512,384]{1,0:T(8,128)(2,1)S(1)} all-gather(bf16[8,384]{1,0:T(8,128)(2,1)S(1)} %copy-done.7), channel_id=1, replica_groups=mesh['dp'=64,'rep'=8] {'dp'}, dimensions={0}, use_global_device_ids=true | all-gather | bytes 399360 | tf_op jit(solution)/shard_map/all_gather | solution.py:76
  244.7 0.0 copy-done.1
  244.7 0.3 convolution_convert_fusion.1
  245.0 0.1 copy.41
  245.1 0.0 copy-done.9
  245.2 0.0 copy-start.8
  245.2 0.0 all-to-all-done
  245.2 0.1 reshape.217
  245.3 1.2 gather_fusion.1
  246.4 0.2 fusion.25
  246.7 0.0 all-gather.2.cloned.1.call-done
  246.7 1.8 convolution_convert_fusion
  248.5 0.2 copy.39
  248.8 1.8 fusion.51
  250.6 1.6 fusion.38
  252.2 0.2 divide_convert_fusion
  252.3 1.0 fusion.10
  253.4 3.1 fusion.8
  256.5 3.2 fusion.9
  259.7 0.3 convolution_convert_fusion.5
  259.9 0.3 convolution_bitcast_fusion
  260.3 0.3 copy-done.4
  260.6 0.1 copy-done.5
  260.7 0.1 copy-done.6
  260.8 0.1 pad_maximum_fusion
  260.9 0.7 fusion.29
  261.5 2.1 maximum_multiply_fusion
  263.6 0.0 reduce-scatter.2.cloned.1.call-update
  263.7 1.6 scatter_custom_fusion
  265.3 1.9 fusion.20
  267.2 0.2 fusion.24
  267.4 1.2 gather_fusion.2
  268.6 0.1 bitcast_select_fusion
  268.7 0.4 copy.54
  269.1 0.5 broadcast.129
  269.6 2.2 reduce.8
  271.8 0.9 reshape.229
  272.7 7.2 all-to-all-start.1
  279.9 1.1 fusion.7
  281.0 13.0 %all-to-all-done.1 = bf16[64,2,1024]{2,1,0:T(2,128)(2,1)S(1)} async-done(((bf16[64,2,1024]{2,1,0:T(2,128)(2,1)}), bf16[64,2,1024]{2,1,0:T(2,128)(2,1)S(1)}, u32[]{:S(2)}, u32[]{:S(2)}) %all-to-all-start.1) | async-done | bytes 262176 | tf_op jit(solution)/shard_map/all_to_all | solution.py:94
  294.0 0.2 reshape.230
  294.2 1.5 bitcast_reduce_fusion
  295.7 0.8 all_to_all.21
  296.5 816.8 %reduce-scatter.2.cloned.1.call-done = f32[8,1536]{1,0:T(8,128)} async-done(((f32[512,1536]{1,0:T(8,128)}), f32[8,1536]{1,0:T(8,128)}) %reduce-scatter.2.cloned.1.call-update) | async-done | bytes 49168 | tf_op jit(solution)/shard_map/reduce_scatter | solution.py:96
  1113.2 0.8 convert_element_type.120
  1114.0 27.2 %psum.7 = bf16[8,1536]{1,0:T(8,128)(2,1)S(1)} all-reduce(bf16[8,1536]{1,0:T(8,128)(2,1)S(1)} %convert_element_type.120), channel_id=1, replica_groups=mesh['dp'=64,'rep'=8] {'rep'}, use_global_device_ids=true, to_apply=%region_8.10 | all-reduce | flops 12288 | bytes 49152 | tf_op jit(solution)/shard_map/psum | solution.py:109
  1141.2 0.6 slice.30
  1141.9 0.6 slice.29
  (18 shorter events, 0.1 us)
Async XLA Ops:
  7.2 1.8 copy-start
  7.2 239.5 %all-gather.2.cloned.1.call-start = ((), (), s32[]{:S(2)}) async-start(), calls=%async_computation.3 | async-start | bytes 1198080 | tf_op jit(solution)/shard_map/all_gather | solution.py:75
  22.9 23.9 %copy-start.7 = (bf16[8,384]{1,0:T(8,128)(2,1)S(1)}, bf16[8,384]{1,0:T(8,128)(2,1)}, u32[]{:S(2)}) copy-start(bf16[8,384]{1,0:T(8,128)(2,1)} %param.14) | copy-start | bytes 18436
  22.9 221.8 %copy-start.1 = (bf16[1,256,512]{2,1,0:T(8,128)(2,1)S(1)}, bf16[1,256,512]{2,1,0:T(8,128)(2,1)}, u32[]{:S(2)}) copy-start(bf16[1,256,512]{2,1,0:T(8,128)(2,1)} %param.15) | copy-start | bytes 786436
  25.3 219.9 %copy-start.9 = (s32[256]{0:T(256)S(1)}, s32[256]{0:T(256)}, u32[]{:S(2)}) copy-start(s32[256]{0:T(256)} %param.11) | copy-start | bytes 3076
  27.1 218.1 %all-to-all-start = ((bf16[64,4,512]{2,1,0:T(4,128)(2,1)}), bf16[64,4,512]{2,1,0:T(4,128)(2,1)S(1)}, u32[]{:S(2)}, u32[]{:S(2)}) async-start(bf16[64,4,512]{2,1,0:T(4,128)(2,1)} %multiply_convert_fusion), calls=%async_computation | async-start | bytes 524288 | tf_op jit(solution)/shard_map/all_to_all | solution.py:63
  46.8 1066.5 %reduce-scatter.2.cloned.1.call-start = ((), (), s32[]{:S(2)}) async-start(), calls=%async_computation.4 | async-start | bytes 3194880 | tf_op jit(solution)/shard_map/reduce_scatter | solution.py:96
  245.2 1.5 copy-start.8
  250.6 1.6 copy-start.3
  256.5 3.4 copy-start.2
  259.7 0.9 copy-start.4
  259.7 1.0 copy-start.5
  259.7 1.1 copy-start.6
  272.7 21.2 %all-to-all-start.1 = ((bf16[64,2,1024]{2,1,0:T(2,128)(2,1)}), bf16[64,2,1024]{2,1,0:T(2,128)(2,1)S(1)}, u32[]{:S(2)}, u32[]{:S(2)}) async-start(bf16[64,2,1024]{2,1,0:T(2,128)(2,1)} %reshape.229), calls=%async_computation.1 | async-start | bytes 524288 | tf_op jit(solution)/shard_map/all_to_all | solution.py:94
Sparse Core Ops, SparseCore 0:
  12.4 132.2 all-gather.1
  263.8 849.4 reduce-scatter.1
where the time goes:
time: 1150 us
  waiting for transfers between devices  831 us (72%)
  blocking collectives  225 us (20%)
  starting transfers between devices  26.9 us (2%)
  local copies, waits for them, and re-layouts  24.7 us (2%)
  matrix products  17 us (1%)
  between operations  14.3 us (1%)
    reduce_scatter x1, waiting for transfers between devices, on_device(): lax.psum_scatter(jnp.concatenate([jnp.dot(hidden.T, grad_projected, prefe...  817 us
    all_gather x1, blocking collectives, on_device(): lax.all_gather(out_weight, 'dp', axis=0, tiled=True)  198 us
    psum x1, blocking collectives, on_device(): lax.psum(owned_rows.astype(jnp.bfloat16), 'rep').astype(jnp.float32)  27.2 us
  transfers between devices with their start and end apart: 4, of which 2 were waited for; matrix products, arithmetic and copies ran while one was open for 3% of the time, Pallas kernels for 0%

commit v1 on v0

v1 whole, which is shorter than its diff:
```python
import jax
import jax.numpy as jnp
from jax import lax
from jax.experimental import pallas as pl
from jax.experimental.pallas import tpu as pltpu
from jax.sharding import PartitionSpec as P

E = 512
H = 6
DH = 64
F = 256
P_SIZE = 4
HD = H * DH
SAMPLES = 512
EPS = 1e-06

NX = 4
NZ = 8
NY = 8
NDP = 64

BF = jnp.bfloat16
F32 = jnp.float32
MESH = pl.DeviceIdType.MESH


def dot(a, b, ca, cb):
    return lax.dot_general(a, b, (((ca,), (cb,)), ((), ())), preferred_element_type=F32)


def fused(
    tables,
    ids,
    slot,
    gain,
    qkv,
    outw,
    cot,
    layer_out,
    pooled_grad,
    grad_qkv,
    grad_out,
    rows_f,
    tok_send,
    tok_recv,
    gt_send,
    gt_recv,
    w_send,
    w_all,
    wq,
    wo,
    g_all,
    sib_recv,
    x_recv,
    s2,
    z_recv,
    s3,
    y_recv,
    fin,
    send_sem,
    recv_sem,
    wx_sem,
    gs_sem,
):
    dp = lax.axis_index("dp")
    rep = lax.axis_index("rep")
    z = dp // 8
    x = lax.rem(dp // 2, 4)
    yh = lax.rem(dp, 2)
    yl = rep // 2
    core = lax.rem(rep, 2)
    other = 1 - core
    y = yh * 4 + yl
    sib = (dp, yl * 2 + other)

    def dp_of(zz, xx, hh):
        return zz * 8 + xx * 2 + hh

    def y_peer(k):
        yy = lax.rem(y + k, NY)
        return yy // 4, (dp_of(z, x, yy // 4), lax.rem(yy, 4) * 2 + core)

    def send(src, dst, ssem, rsem, who):
        pltpu.make_async_remote_copy(
            src_ref=src,
            dst_ref=dst,
            send_sem=ssem,
            recv_sem=rsem,
            device_id=who,
            device_id_type=MESH,
        ).start()

    def drain(ref, sem):
        pltpu.make_async_copy(ref, ref, sem).wait()

    barrier = pltpu.get_barrier_semaphore()

    def greet(k, carry):
        pl.semaphore_signal(
            barrier, inc=1, device_id=(lax.rem(dp + k, NDP), rep), device_id_type=MESH
        )
        return carry

    lax.fori_loop(1, NDP, greet, 0)
    pl.semaphore_signal(barrier, inc=1, device_id=sib, device_id_type=MESH)
    for k in range(1, NY):
        pl.semaphore_signal(barrier, inc=1, device_id=y_peer(k)[1], device_id_type=MESH)

    wide = jnp.concatenate([qkv[...].astype(F32), outw[...].astype(F32)], axis=1)
    for k in range(6):
        pair = jnp.concatenate(
            [wide[:, 256 * k : 256 * k + 128], wide[:, 256 * k + 128 : 256 * k + 256]], axis=0
        ).astype(BF)
        w_send[k // 3, 16 * (k % 3) : 16 * (k % 3) + 16, :] = pair
    w_all[core, x, z * 2 + yh] = w_send[core]

    row_iota = lax.broadcasted_iota(jnp.int32, (F, NDP), 0)
    for j in range(4):
        counts = jnp.zeros((F, NDP), F32)
        for p in range(P_SIZE):
            counts = counts + jnp.where(row_iota == ids[4 * j + p : 4 * j + p + 1, :], 1.0, 0.0)
        pooled = dot(counts.astype(BF), tables[j], 0, 0) * 0.5
        for cb in range(4):
            rows_f[pl.ds(4 * j + cb, NDP, stride=16), :] = pooled[:, 128 * cb : 128 * cb + 128]
    tok_send[...] = rows_f[...].astype(BF).reshape(NDP, 16, 128)
    tok_recv[dp] = tok_send[dp]

    pl.semaphore_wait(barrier, NDP - 1 + 1 + NY - 1)

    for k in range(1, 16):
        q = lax.rem(z * 2 + yh + k, 16)
        send(
            w_send.at[core],
            w_all.at[core, x, z * 2 + yh],
            send_sem.at[0],
            recv_sem.at[0],
            (dp_of(q // 2, x, lax.rem(q, 2)), rep),
        )

    def send_tok(k, carry):
        p = lax.rem(dp + k, NDP)
        send(tok_send.at[p], tok_recv.at[dp], send_sem.at[1], recv_sem.at[1], (p, rep))
        return carry

    lax.fori_loop(1, NDP, send_tok, 0)

    drain(w_all.at[core, x, pl.ds(0, 15)], recv_sem.at[0])
    for k in (1, 3, 2):
        send(
            w_all.at[core, x],
            w_all.at[core, x],
            send_sem.at[2],
            wx_sem.at[k - 1],
            (dp_of(z, lax.rem(x + k, NX), yh), rep),
        )
    send(w_all.at[core, x], w_all.at[core, x], send_sem.at[3], recv_sem.at[2], sib)
    for k in (1, 3, 2):
        xx = lax.rem(x + NX - k, NX)
        drain(w_all.at[core, xx], wx_sem.at[k - 1])
        send(w_all.at[core, xx], w_all.at[core, xx], send_sem.at[3], recv_sem.at[2], sib)

    drain(tok_recv.at[pl.ds(0, NDP - 1)], recv_sem.at[1])
    rows_f[...] = tok_recv[...].reshape(NDP * 16, 128).astype(F32)
    by_slot = jnp.concatenate(
        [rows_f[pl.ds(cb, F, stride=4), :] for cb in range(4)], axis=1
    ).astype(BF)
    slot_iota = lax.broadcasted_iota(jnp.int32, (F, F), 0)
    place = jnp.where(slot_iota == slot[...], 1.0, 0.0).astype(BF)
    tokens = dot(place, by_slot, 0, 0)
    inv = lax.rsqrt(jnp.mean(tokens * tokens, axis=-1, keepdims=True) + EPS)
    normed = tokens * inv
    gains = gain[...]
    hidden = (normed * gains).astype(BF)

    drain(w_all.at[other], recv_sem.at[2])
    for k in range(6):
        c, part = k // 3, k % 3
        for xx in range(NX):
            both = w_all[c, xx, :, 16 * part : 16 * part + 16, :].astype(F32)
            both = both.reshape(NZ, 2, 2, 8, 128)
            for half in range(2):
                block = both[:, :, half].reshape(NZ, 16, 128).astype(BF)
                cb = 2 * k + half
                for zz in range(NZ):
                    r0 = 64 * zz + 16 * xx
                    if cb < 9:
                        wq[r0 : r0 + 16, 128 * cb : 128 * cb + 128] = block[zz]
                    else:
                        wo[r0 : r0 + 16, 128 * (cb - 9) : 128 * (cb - 9) + 128] = block[zz]

    grad_context = dot(cot[...], wo[...], 1, 0).astype(BF)
    projected = dot(hidden, wq[...], 1, 0).astype(BF)
    low = lax.broadcasted_iota(jnp.int32, (F, 128), 1) < DH
    zero = jnp.zeros((F, 128), BF)
    contexts, gq, gk, gv = [], [], [], []
    for i in range(H // 2):
        q2 = projected[:, 128 * i : 128 * i + 128]
        k2 = projected[:, HD + 128 * i : HD + 128 * i + 128]
        v2 = projected[:, 2 * HD + 128 * i : 2 * HD + 128 * i + 128]
        c2 = grad_context[:, 128 * i : 128 * i + 128]
        parts = []
        for half in range(2):
            mine = low if half == 0 else jnp.logical_not(low)
            scores = dot(jnp.where(mine, q2, zero), k2, 1, 1) * DH ** (-0.5)
            raised = jnp.exp(scores - jnp.max(scores, axis=-1, keepdims=True))
            soft = (raised / jnp.sum(raised, axis=-1, keepdims=True)).astype(BF)
            context = dot(soft, v2, 1, 0)
            grad_soft = dot(jnp.where(mine, c2, zero), v2, 1, 1)
            soft_f = soft.astype(F32)
            inner = jnp.sum(soft_f * grad_soft, axis=-1, keepdims=True)
            gs = (soft_f * (grad_soft - inner) * DH ** (-0.5)).astype(BF)
            parts.append((context, dot(gs, k2, 1, 0), dot(gs, q2, 0, 0), dot(soft, c2, 0, 0)))
        for out, a, b in zip((contexts, gq, gk, gv), parts[0], parts[1]):
            out.append(jnp.where(low, a, b).astype(BF))
    context = jnp.concatenate(contexts, axis=1)
    grad_projected = jnp.concatenate(gq + gk + gv, axis=1)

    for k in range(6):
        c, part = k // 3, k % 3
        blocks = []
        for cb in (2 * k, 2 * k + 1):
            if cb < 9:
                g = dot(hidden, grad_projected[:, 128 * cb : 128 * cb + 128], 0, 0)
            else:
                g = dot(cot[...], context[:, 128 * (cb - 9) : 128 * (cb - 9) + 128], 0, 0)
            blocks.append(g.reshape(NZ, NX, 2, 8, 128))
        both = jnp.concatenate(blocks, axis=3).astype(BF)
        for xx in range(NX):
            g_all[c, xx, :, 16 * part : 16 * part + 16, :] = both[:, xx].reshape(16, 16, 128)

    for k in range(NX):
        xx = lax.rem(x + 1 + k, NX)
        send(g_all.at[other, xx], sib_recv.at[xx], send_sem.at[4], gs_sem.at[k], sib)

    layer_out[...] = (tokens + dot(context, wo[...], 1, 1)).astype(BF)
    scaled = dot(grad_projected, wq[...], 1, 1) * gains
    grad_norm = inv * (scaled - normed * jnp.mean(scaled * normed, axis=-1, keepdims=True))
    grad_tokens = (cot[...].astype(F32) + grad_norm).astype(BF)
    grad_slots = dot(place, grad_tokens, 1, 0)
    for cb in range(4):
        rows_f[pl.ds(cb, F, stride=4), :] = grad_slots[:, 128 * cb : 128 * cb + 128]
    gt_send[...] = rows_f[...].astype(BF).reshape(NDP, 16, 128)

    for k in range(NX):
        xx = lax.rem(x + 1 + k, NX)
        drain(sib_recv.at[xx], gs_sem.at[k])
        total = g_all[core, xx].astype(F32) + sib_recv[xx].astype(F32)
        if k < NX - 1:
            g_all[core, xx] = total.astype(BF)
            send(
                g_all.at[core, xx],
                x_recv.at[k],
                send_sem.at[5],
                recv_sem.at[3],
                (dp_of(z, xx, yh), rep),
            )

    def send_grad(k, carry):
        p = lax.rem(dp + k, NDP)
        send(gt_send.at[p], gt_recv.at[dp], send_sem.at[6], recv_sem.at[4], (p, rep))
        return carry

    lax.fori_loop(1, NDP, send_grad, 0)
    gt_recv[dp] = gt_send[dp]

    drain(x_recv, recv_sem.at[3])
    for k in range(NX - 1):
        total = total + x_recv[k].astype(F32)
    s2[...] = total.astype(BF).reshape(NZ, 2, 48, 128)

    for k in range(1, NZ):
        zz = lax.rem(z + k, NZ)
        send(
            s2.at[zz], z_recv.at[k - 1], send_sem.at[7], recv_sem.at[5], (dp_of(zz, x, yh), rep)
        )
    total = s2[z].astype(F32)
    drain(z_recv, recv_sem.at[5])
    for k in range(NZ - 1):
        total = total + z_recv[k].astype(F32)
    s3[...] = total.astype(BF)

    for k in range(1, NY):
        hh, who = y_peer(k)
        send(s3.at[hh], y_recv.at[k - 1], send_sem.at[8], recv_sem.at[6], who)
    total = s3[yh].astype(F32)
    drain(y_recv, recv_sem.at[6])
    for k in range(NY - 1):
        total = total + y_recv[k].astype(F32)
    fin[core] = total * (1.0 / SAMPLES)
    send(fin.at[core], fin.at[core], send_sem.at[9], recv_sem.at[7], sib)

    drain(gt_recv.at[pl.ds(0, NDP - 1)], recv_sem.at[4])
    pooled_grad[...] = gt_recv[...]
    drain(fin.at[other], recv_sem.at[7])
    for cb in range(12):
        piece = fin[cb // 6, 8 * (cb % 6) : 8 * (cb % 6) + 8, :]
        if cb < 9:
            grad_qkv[:, 128 * cb : 128 * cb + 128] = piece
        else:
            grad_out[:, 128 * (cb - 9) : 128 * (cb - 9) + 128] = piece

    drain(w_all.at[core, x, pl.ds(0, 15)], send_sem.at[0])
    drain(tok_send.at[pl.ds(0, NDP - 1)], send_sem.at[1])
    drain(w_all.at[core, pl.ds(0, 3)], send_sem.at[2])
    drain(w_all.at[core], send_sem.at[3])
    drain(sib_recv, send_sem.at[4])
    drain(x_recv, send_sem.at[5])
    drain(gt_send.at[pl.ds(0, NDP - 1)], send_sem.at[6])
    drain(z_recv, send_sem.at[7])
    drain(y_recv, send_sem.at[8])
    drain(fin.at[core], send_sem.at[9])


def on_device(tables, sample_ids, table_slot, norm_gain, qkv_weight, out_weight, cotangent):
    vmem = pl.BlockSpec(memory_space=pltpu.VMEM)
    layer_out, pooled_grad, grad_qkv, grad_out = pl.pallas_call(
        fused,
        out_shape=(
            jax.ShapeDtypeStruct((F, E), BF),
            jax.ShapeDtypeStruct((NDP, 16, 128), BF),
            jax.ShapeDtypeStruct((8, 3 * HD), F32),
            jax.ShapeDtypeStruct((8, HD), F32),
        ),
        in_specs=[vmem] * 7,
        out_specs=(vmem,) * 4,
        scratch_shapes=[
            pltpu.VMEM((NDP * 16, 128), F32),
            pltpu.VMEM((NDP, 16, 128), BF),
            pltpu.VMEM((NDP, 16, 128), BF),
            pltpu.VMEM((NDP, 16, 128), BF),
            pltpu.VMEM((NDP, 16, 128), BF),
            pltpu.VMEM((2, 48, 128), BF),
            pltpu.VMEM((2, NX, 16, 48, 128), BF),
            pltpu.VMEM((E, 3 * HD), BF),
            pltpu.VMEM((E, HD), BF),
            pltpu.VMEM((2, NX, 16, 48, 128), BF),
            pltpu.VMEM((NX, 16, 48, 128), BF),
            pltpu.VMEM((NX - 1, 16, 48, 128), BF),
            pltpu.VMEM((NZ, 2, 48, 128), BF),
            pltpu.VMEM((NZ - 1, 2, 48, 128), BF),
            pltpu.VMEM((2, 48, 128), BF),
            pltpu.VMEM((NY - 1, 48, 128), BF),
            pltpu.VMEM((2, 48, 128), F32),
            pltpu.SemaphoreType.DMA((10,)),
            pltpu.SemaphoreType.DMA((8,)),
            pltpu.SemaphoreType.DMA((3,)),
            pltpu.SemaphoreType.DMA((4,)),
        ],
        compiler_params=pltpu.CompilerParams(
            collective_id=0, has_side_effects=True, vmem_limit_bytes=48 * 1024 * 1024
        ),
        cost_estimate=pl.CostEstimate(
            flops=2_000_000_000, bytes_accessed=4_000_000, transcendentals=400_000
        ),
    )(
        tables,
        jnp.transpose(sample_ids, (1, 2, 0)).reshape(16, NDP),
        table_slot.reshape(1, F),
        norm_gain.reshape(1, E),
        qkv_weight,
        out_weight,
        cotangent.reshape(F, E),
    )
    return (
        layer_out.reshape(1, F, E),
        pooled_grad.reshape(NDP, 4, E),
        grad_qkv,
        grad_out,
    )


def solution(mesh):
    return jax.shard_map(
        on_device,
        mesh=mesh,
        in_specs=(
            P("dp", None, None),
            P("rep", "dp", None),
            P(),
            P(),
            P("dp", None),
            P("dp", None),
            P(("rep", "dp"), None, None),
        ),
        out_specs=(
            P(("rep", "dp"), None, None),
            P("rep", "dp", None),
            P("dp", None),
            P("dp", None),
        ),
        check_vma=False,
    )
```

time: 1150 us -> 82.3 us (0.07)
  waiting for transfers between devices: 831 us -> 0 us
  blocking collectives: 225 us -> 0 us
  Pallas kernels: 0 us -> 73.6 us
  starting transfers between devices: 26.9 us -> 0 us
  local copies, waits for them, and re-layouts: 24.7 us -> 7.67 us
  matrix products: 17 us -> 0 us
  between operations: 14.3 us -> 0.66 us
    reduce_scatter x1 -> x0, waiting for transfers between devices: 817 us -> none  [on_device(): lax.psum_scatter(jnp.concatenate([jnp.dot(hidden.T, grad_projected, prefe...]
    all_gather x1 -> x0, blocking collectives: 198 us -> none  [on_device(): lax.all_gather(out_weight, 'dp', axis=0, tiled=True)]
    pallas_call x0 -> x1, Pallas kernels: none -> 73.6 us  [on_device(): pl.pallas_call(fused, out_shape=(jax.ShapeDtypeStruct((F, E), BF), jax.Sh...]
    psum x1 -> x0, blocking collectives: 27.2 us -> none  [on_device(): lax.psum(owned_rows.astype(jnp.bfloat16), 'rep').astype(jnp.float32)]
    all_to_all x2 -> x0, starting transfers between devices: 26.8 us -> none  [the longest x1 19.6 us: on_device(): lax.all_to_all(pooled, 'dp', split_axis=0, concat_axis=1, tiled=True)]
    dot_general x11 -> x0, matrix products: 15.2 us -> none  [the longest x1 3.16 us: attend_back(): jnp.einsum('shqk,sqhd->skhd', grad_scores, query_part, preferred_element_...]
    gather x3 -> x0, local copies, waits for them, and re-layouts: 14.6 us -> none  [the longest x1 12.3 us: on_device(): gathered = tables[slot_index, sample_ids]]
    all_to_all x2 -> x0, waiting for transfers between devices: 13 us -> none  [the longest x1 13 us: on_device(): lax.all_to_all(grad_slots, 'dp', split_axis=1, concat_axis=0, tiled=True)]
  transfers between devices with their start and end apart: 4 -> 0, of which waited for: 2 -> 0; matrix products, arithmetic and copies ran while one was open for 3% -> 0% of each run, Pallas kernels for 0% -> 0%
where the time goes in v1:
time: 82.3 us; the launch traced here: 81.9 us
  Pallas kernels  73.6 us (89%)
  local copies, waits for them, and re-layouts  7.67 us (9%)
    pallas_call x1, Pallas kernels, on_device(): pl.pallas_call(fused, out_shape=(jax.ShapeDtypeStruct((F, E), BF), jax.Sh...  73.6 us
    unnamed x17, local copies, waits for them, and re-layouts  6.87 us

profile of v1, /device:TPU:1, one launch (start us, length us, event | category | flops | bytes accessed | tf_op | source)
XLA Modules:
  0.0 81.9 jit_solution(7546126528172663710)
XLA Ops:
  0.6 0.0 copy-start.4
  0.6 0.0 copy-start.6
  0.7 0.7 copy-done.4
  1.3 0.0 copy-done.6
  1.3 0.0 copy-start
  1.3 1.2 %copy-done = bf16[4,256,512]{2,1,0:T(8,128)(2,1)S(1)} copy-done((bf16[4,256,512]{2,1,0:T(8,128)(2,1)S(1)}, bf16[4,256,512]{2,1,0:T(8,128)(2,1)}, u32[]{:S(2)}) %copy-start) | copy-done | bytes 1048600
  2.6 0.0 copy-start.1
  2.6 0.9 %copy-done.1 = bf16[1,256,512]{2,1,0:T(8,128)(2,1)S(1)} copy-done((bf16[1,256,512]{2,1,0:T(8,128)(2,1)S(1)}, bf16[1,256,512]{2,1,0:T(8,128)(2,1)}, u32[]{:S(2)}) %copy-start.1) | copy-done | bytes 262168
  3.5 0.0 copy-start.2
  3.5 0.7 copy-done.2
  4.2 0.0 copy-start.3
  4.2 0.7 copy-done.3
  4.9 0.0 copy-start.5
  4.9 0.7 copy-done.5
  5.6 73.6 %shard_map.102 = (bf16[256,512]{1,0:T(8,128)(2,1)S(1)}, bf16[64,16,128]{2,1,0:T(8,128)(2,1)S(1)}, f32[8,1152]{1,0:T(8,128)S(1)}, f32[8,384]{1,0:T(8,128)S(1)}) custom-call(bf16[4,256,512]{2,1,0:T(8,128)(2,1)S(1)} %copy-done, s32[16,64]{1,0:T(8,128)S(1)} %bitcast.9, s32[1,256]{1,0:T(1,128)S(1)} %bitcast.11, f32[1,512]{1,0:T(1,128)S(1)} %bitcast.10, ...), custom_call_target="tpu_custom_call" | custom-call | flops 2000000000 | bytes 4000000 | tf_op jit(solution)/shard_map/pallas_call | solution.py:316
  79.2 0.8 reshape.31
  80.0 0.7 copy.14
  80.7 0.6 copy.15
  81.3 0.6 copy.16
Async XLA Ops:
  0.6 0.7 copy-start.4
  0.6 0.7 copy-start.6
  1.3 1.2 %copy-start = (bf16[4,256,512]{2,1,0:T(8,128)(2,1)S(1)}, bf16[4,256,512]{2,1,0:T(8,128)(2,1)}, u32[]{:S(2)}) copy-start(bf16[4,256,512]{2,1,0:T(8,128)(2,1)} %tables.1) | copy-start | bytes 3145732
  2.6 0.9 %copy-start.1 = (bf16[1,256,512]{2,1,0:T(8,128)(2,1)S(1)}, bf16[1,256,512]{2,1,0:T(8,128)(2,1)}, u32[]{:S(2)}) copy-start(bf16[1,256,512]{2,1,0:T(8,128)(2,1)} %param.13) | copy-start | bytes 786436
  3.5 0.7 copy-start.2
  4.2 0.7 copy-start.3
  4.9 0.7 copy-start.5

commit v2 on v1

v2 whole, which is shorter than its diff:
```python
import jax
import jax.numpy as jnp
from jax import lax
from jax.experimental import pallas as pl
from jax.experimental.pallas import tpu as pltpu
from jax.sharding import PartitionSpec as P

E = 512
H = 6
DH = 64
F = 256
P_SIZE = 4
HD = H * DH
SAMPLES = 512
EPS = 1e-06

NX = 4
NZ = 8
NY = 8
NDP = 64

BF = jnp.bfloat16
F32 = jnp.float32
MESH = pl.DeviceIdType.MESH


def dot(a, b, ca, cb):
    return lax.dot_general(a, b, (((ca,), (cb,)), ((), ())), preferred_element_type=F32)


def fused(
    tables_h,
    ids_h,
    slot_h,
    gain_h,
    qkv,
    outw,
    cot_h,
    layer_out_h,
    pooled_grad_h,
    grad_qkv_h,
    grad_out_h,
    tables,
    ids,
    slot,
    gain,
    cot,
    rows_f,
    tok_send,
    tok_recv,
    gt_send,
    gt_recv,
    w_send,
    w_all,
    wq,
    wo,
    g_all,
    sib_recv,
    x_recv,
    s2,
    z_recv,
    s3,
    y_recv,
    fin,
    send_sem,
    recv_sem,
    w_sem,
    wx_sem,
    ws_sem,
    sib_sem,
    x_sem,
    z_sem,
    y_sem,
    fin_sem,
    in_sem,
    layer_out,
    grad_qkv,
    grad_out,
    out_sem,
):
    dp = lax.axis_index("dp")
    rep = lax.axis_index("rep")
    z = dp // 8
    x = lax.rem(dp // 2, 4)
    yh = lax.rem(dp, 2)
    yl = rep // 2
    core = lax.rem(rep, 2)
    other = 1 - core
    y = yh * 4 + yl
    sib = (dp, yl * 2 + other)

    def dp_of(zz, xx, hh):
        return zz * 8 + xx * 2 + hh

    def y_peer(k):
        yy = lax.rem(y + k, NY)
        return yy // 4, (dp_of(z, x, yy // 4), lax.rem(yy, 4) * 2 + core)

    def send(src, dst, ssem, rsem, who):
        pltpu.make_async_remote_copy(
            src_ref=src,
            dst_ref=dst,
            send_sem=ssem,
            recv_sem=rsem,
            device_id=who,
            device_id_type=MESH,
        ).start()

    def drain(ref, sem):
        pltpu.make_async_copy(ref, ref, sem).wait()

    barrier = pltpu.get_barrier_semaphore()

    def greet(k, carry):
        pl.semaphore_signal(
            barrier, inc=1, device_id=(lax.rem(dp + k, NDP), rep), device_id_type=MESH
        )
        return carry

    lax.fori_loop(1, NDP, greet, 0)
    pl.semaphore_signal(barrier, inc=1, device_id=sib, device_id_type=MESH)
    for k in range(1, NY):
        pl.semaphore_signal(barrier, inc=1, device_id=y_peer(k)[1], device_id_type=MESH)

    def load(i, src, dst):
        pltpu.make_async_copy(src, dst, in_sem.at[i]).start()

    def loaded(i, src, dst):
        pltpu.make_async_copy(src, dst, in_sem.at[i]).wait()

    inputs = (
        (ids_h, ids),
        (tables_h, tables),
        (slot_h, slot),
        (gain_h, gain),
        (cot_h, cot),
    )
    for i, (src, dst) in enumerate(inputs):
        load(i, src, dst)

    wide = jnp.concatenate([qkv[...].astype(F32), outw[...].astype(F32)], axis=1)
    for k in range(6):
        pair = jnp.concatenate(
            [wide[:, 256 * k : 256 * k + 128], wide[:, 256 * k + 128 : 256 * k + 256]], axis=0
        ).astype(BF)
        w_send[k // 3, k % 3] = pair
    for part in range(3):
        w_all[core, part, x, z * 2 + yh] = w_send[core, part]

    pl.semaphore_wait(barrier, NDP - 1 + 1 + NY - 1)

    for part in range(3):
        for k in range(1, 16):
            q = lax.rem(z * 2 + yh + k, 16)
            send(
                w_send.at[core, part],
                w_all.at[core, part, x, z * 2 + yh],
                send_sem.at[0],
                w_sem.at[part],
                (dp_of(q // 2, x, lax.rem(q, 2)), rep),
            )

    loaded(0, *inputs[0])
    loaded(1, *inputs[1])
    row_iota = lax.broadcasted_iota(jnp.int32, (F, NDP), 0)
    for j in range(4):
        counts = jnp.zeros((F, NDP), F32)
        for p in range(P_SIZE):
            counts = counts + jnp.where(row_iota == ids[4 * j + p : 4 * j + p + 1, :], 1.0, 0.0)
        pooled = dot(counts.astype(BF), tables[j], 0, 0) * 0.5
        for cb in range(4):
            rows_f[pl.ds(4 * j + cb, NDP, stride=16), :] = pooled[:, 128 * cb : 128 * cb + 128]
    tok_send[...] = rows_f[...].astype(BF).reshape(NDP, 16, 128)
    tok_recv[dp] = tok_send[dp]

    def send_tok(k, carry):
        p = lax.rem(dp + k, NDP)
        send(tok_send.at[p], tok_recv.at[dp], send_sem.at[1], recv_sem.at[1], (p, rep))
        return carry

    lax.fori_loop(1, NDP, send_tok, 0)

    def to_sibling(part, xx):
        block = w_all.at[core, part, xx]
        send(block, block, send_sem.at[3], ws_sem.at[part], sib)

    def forward(part):
        for k in (1, 3, 2):
            xx = lax.rem(x + NX - k, NX)
            drain(w_all.at[core, part, xx], wx_sem.at[part, k - 1])
            to_sibling(part, xx)

    for part in range(3):
        block = w_all.at[core, part, x]
        drain(w_all.at[core, part, x, pl.ds(0, 15)], w_sem.at[part])
        for k in (1, 3, 2):
            send(
                block,
                block,
                send_sem.at[2],
                wx_sem.at[part, k - 1],
                (dp_of(z, lax.rem(x + k, NX), yh), rep),
            )
        to_sibling(part, x)
    forward(0)
    forward(1)

    drain(tok_recv.at[pl.ds(0, NDP - 1)], recv_sem.at[1])
    rows_f[...] = tok_recv[...].reshape(NDP * 16, 128).astype(F32)
    by_slot = jnp.concatenate(
        [rows_f[pl.ds(cb, F, stride=4), :] for cb in range(4)], axis=1
    ).astype(BF)
    loaded(2, *inputs[2])
    loaded(3, *inputs[3])
    slot_iota = lax.broadcasted_iota(jnp.int32, (F, F), 0)
    place = jnp.where(slot_iota == slot[...], 1.0, 0.0).astype(BF)
    tokens = dot(place, by_slot, 0, 0)
    inv = lax.rsqrt(jnp.mean(tokens * tokens, axis=-1, keepdims=True) + EPS)
    normed = tokens * inv
    gains = gain[...]
    hidden = (normed * gains).astype(BF)

    forward(2)
    for part in range(3):
        drain(w_all.at[other, part], ws_sem.at[part])
        for k in (part, part + 3):
            for xx in range(NX):
                both = w_all[k // 3, part, xx].astype(F32).reshape(NZ, 2, 2, 8, 128)
                for half in range(2):
                    block = both[:, :, half].reshape(NZ, 16, 128).astype(BF)
                    cb = 2 * k + half
                    for zz in range(NZ):
                        r0 = 64 * zz + 16 * xx
                        if cb < 9:
                            wq[r0 : r0 + 16, 128 * cb : 128 * cb + 128] = block[zz]
                        else:
                            wo[r0 : r0 + 16, 128 * (cb - 9) : 128 * (cb - 9) + 128] = block[zz]

    loaded(4, *inputs[4])
    grad_context = dot(cot[...], wo[...], 1, 0).astype(BF)
    projected = dot(hidden, wq[...], 1, 0).astype(BF)
    low = lax.broadcasted_iota(jnp.int32, (F, 128), 1) < DH
    zero = jnp.zeros((F, 128), BF)
    contexts, gq, gk, gv = [], [], [], []
    for i in range(H // 2):
        q2 = projected[:, 128 * i : 128 * i + 128]
        k2 = projected[:, HD + 128 * i : HD + 128 * i + 128]
        v2 = projected[:, 2 * HD + 128 * i : 2 * HD + 128 * i + 128]
        c2 = grad_context[:, 128 * i : 128 * i + 128]
        parts = []
        for half in range(2):
            mine = low if half == 0 else jnp.logical_not(low)
            scores = dot(jnp.where(mine, q2, zero), k2, 1, 1) * DH ** (-0.5)
            raised = jnp.exp(scores - jnp.max(scores, axis=-1, keepdims=True))
            soft = (raised / jnp.sum(raised, axis=-1, keepdims=True)).astype(BF)
            context = dot(soft, v2, 1, 0)
            grad_soft = dot(jnp.where(mine, c2, zero), v2, 1, 1)
            soft_f = soft.astype(F32)
            inner = jnp.sum(soft_f * grad_soft, axis=-1, keepdims=True)
            gs = (soft_f * (grad_soft - inner) * DH ** (-0.5)).astype(BF)
            parts.append((context, dot(gs, k2, 1, 0), dot(gs, q2, 0, 0), dot(soft, c2, 0, 0)))
        for out, a, b in zip((contexts, gq, gk, gv), parts[0], parts[1]):
            out.append(jnp.where(low, a, b).astype(BF))
    context = jnp.concatenate(contexts, axis=1)
    grad_projected = jnp.concatenate(gq + gk + gv, axis=1)

    for part in range(3):
        for c in range(2):
            k = 3 * c + part
            blocks = []
            for cb in (2 * k, 2 * k + 1):
                if cb < 9:
                    g = dot(hidden, grad_projected[:, 128 * cb : 128 * cb + 128], 0, 0)
                else:
                    g = dot(cot[...], context[:, 128 * (cb - 9) : 128 * (cb - 9) + 128], 0, 0)
                blocks.append(g.reshape(NZ, NX, 2, 8, 128))
            both = jnp.concatenate(blocks, axis=3).astype(BF)
            for xx in range(NX):
                g_all[c, part, xx] = both[:, xx].reshape(16, 16, 128)
        send(g_all.at[other, part], sib_recv.at[part], send_sem.at[4], sib_sem.at[part], sib)

    scaled = dot(grad_projected, wq[...], 1, 1) * gains
    grad_norm = inv * (scaled - normed * jnp.mean(scaled * normed, axis=-1, keepdims=True))
    grad_tokens = (cot[...].astype(F32) + grad_norm).astype(BF)
    turned = lax.rem(slot_iota, NDP) * 4 + slot_iota // NDP
    place_back = jnp.where(turned == slot[...], 1.0, 0.0).astype(BF)
    grad_slots = dot(place_back, grad_tokens, 1, 0)
    for cb in range(4):
        for j in range(4):
            rows_f[pl.ds(4 * cb + j, NDP, stride=16), :] = grad_slots[
                NDP * j : NDP * j + NDP, 128 * cb : 128 * cb + 128
            ]
    gt_send[...] = rows_f[...].astype(BF).reshape(NDP, 16, 128)

    def send_grad(k, carry):
        p = lax.rem(dp + k, NDP)
        send(gt_send.at[p], gt_recv.at[dp], send_sem.at[6], recv_sem.at[4], (p, rep))
        return carry

    lax.fori_loop(1, NDP, send_grad, 0)
    gt_recv[dp] = gt_send[dp]

    mine = []
    for part in range(3):
        drain(sib_recv.at[part], sib_sem.at[part])
        for k in range(NX):
            xx = lax.rem(x + 1 + k, NX)
            total = g_all[core, part, xx].astype(F32) + sib_recv[part, xx].astype(F32)
            if k < NX - 1:
                g_all[core, part, xx] = total.astype(BF)
                send(
                    g_all.at[core, part, xx],
                    x_recv.at[part, k],
                    send_sem.at[5],
                    x_sem.at[part],
                    (dp_of(z, xx, yh), rep),
                )
        mine.append(total)

    layer_out[...] = (tokens + dot(context, wo[...], 1, 1)).astype(BF)
    outputs = (
        (layer_out, layer_out_h),
        (gt_recv, pooled_grad_h),
        (grad_qkv, grad_qkv_h),
        (grad_out, grad_out_h),
    )

    def store(i):
        return pltpu.make_async_copy(*outputs[i], out_sem.at[i])

    store(0).start()

    for part in range(3):
        drain(x_recv.at[part], x_sem.at[part])
        total = mine[part]
        for k in range(NX - 1):
            total = total + x_recv[part, k].astype(F32)
        s2[part] = total.astype(BF).reshape(NZ, 2, 16, 128)
        for k in range(1, NZ):
            zz = lax.rem(z + k, NZ)
            send(
                s2.at[part, zz],
                z_recv.at[part, k - 1],
                send_sem.at[7],
                z_sem.at[part],
                (dp_of(zz, x, yh), rep),
            )

    for part in range(3):
        total = s2[part, z].astype(F32)
        drain(z_recv.at[part], z_sem.at[part])
        for k in range(NZ - 1):
            total = total + z_recv[part, k].astype(F32)
        s3[part] = total.astype(BF)
        for k in range(1, NY):
            hh, who = y_peer(k)
            send(s3.at[part, hh], y_recv.at[part, k - 1], send_sem.at[8], y_sem.at[part], who)
    drain(gt_recv.at[pl.ds(0, NDP - 1)], recv_sem.at[4])
    store(1).start()
    for part in range(3):
        total = s3[part, yh].astype(F32)
        drain(y_recv.at[part], y_sem.at[part])
        for k in range(NY - 1):
            total = total + y_recv[part, k].astype(F32)
        fin[core, part] = total * (1.0 / SAMPLES)
    send(fin.at[core], fin.at[core], send_sem.at[9], fin_sem.at[0], sib)

    drain(fin.at[other], fin_sem.at[0])
    for cb in range(12):
        piece = fin[cb // 6, (cb % 6) // 2, 8 * (cb % 2) : 8 * (cb % 2) + 8, :]
        if cb < 9:
            grad_qkv[:, 128 * cb : 128 * cb + 128] = piece
        else:
            grad_out[:, 128 * (cb - 9) : 128 * (cb - 9) + 128] = piece
    store(2).start()
    store(3).start()

    drain(w_all.at[core, pl.ds(0, 3), x, pl.ds(0, 15)], send_sem.at[0])
    drain(tok_send.at[pl.ds(0, NDP - 1)], send_sem.at[1])
    drain(w_all.at[core, pl.ds(0, 3), pl.ds(0, 3)], send_sem.at[2])
    drain(w_all.at[core], send_sem.at[3])
    drain(sib_recv, send_sem.at[4])
    drain(x_recv, send_sem.at[5])
    drain(gt_send.at[pl.ds(0, NDP - 1)], send_sem.at[6])
    drain(z_recv, send_sem.at[7])
    drain(y_recv, send_sem.at[8])
    drain(fin.at[core], send_sem.at[9])
    for i in range(4):
        store(i).wait()


def finish(layer_in, pooled_in, qkv_in, out_in, layer_out, pooled_grad, grad_qkv, grad_out):
    layer_out[...] = layer_in[...]
    grad_qkv[...] = qkv_in[...]
    grad_out[...] = out_in[...]
    for cb in range(4):
        pooled_grad[:, :, 128 * cb : 128 * cb + 128] = pooled_in[:, 4 * cb : 4 * cb + 4, :]


def on_device(tables, sample_ids, table_slot, norm_gain, qkv_weight, out_weight, cotangent):
    vmem = pl.BlockSpec(memory_space=pltpu.VMEM)
    hbm = pl.BlockSpec(memory_space=pltpu.HBM)
    results = pl.pallas_call(
        fused,
        out_shape=(
            jax.ShapeDtypeStruct((F, E), BF),
            jax.ShapeDtypeStruct((NDP, 16, 128), BF),
            jax.ShapeDtypeStruct((8, 3 * HD), F32),
            jax.ShapeDtypeStruct((8, HD), F32),
        ),
        in_specs=[hbm] * 4 + [vmem] * 2 + [hbm],
        out_specs=(hbm,) * 4,
        scratch_shapes=[
            pltpu.VMEM((4, F, E), BF),
            pltpu.VMEM((16, NDP), jnp.int32),
            pltpu.VMEM((1, F), jnp.int32),
            pltpu.VMEM((1, E), F32),
            pltpu.VMEM((F, E), BF),
            pltpu.VMEM((NDP * 16, 128), F32),
            pltpu.VMEM((NDP, 16, 128), BF),
            pltpu.VMEM((NDP, 16, 128), BF),
            pltpu.VMEM((NDP, 16, 128), BF),
            pltpu.VMEM((NDP, 16, 128), BF),
            pltpu.VMEM((2, 3, 16, 128), BF),
            pltpu.VMEM((2, 3, NX, 16, 16, 128), BF),
            pltpu.VMEM((E, 3 * HD), BF),
            pltpu.VMEM((E, HD), BF),
            pltpu.VMEM((2, 3, NX, 16, 16, 128), BF),
            pltpu.VMEM((3, NX, 16, 16, 128), BF),
            pltpu.VMEM((3, NX - 1, 16, 16, 128), BF),
            pltpu.VMEM((3, NZ, 2, 16, 128), BF),
            pltpu.VMEM((3, NZ - 1, 2, 16, 128), BF),
            pltpu.VMEM((3, 2, 16, 128), BF),
            pltpu.VMEM((3, NY - 1, 16, 128), BF),
            pltpu.VMEM((2, 3, 16, 128), F32),
            pltpu.SemaphoreType.DMA((10,)),
            pltpu.SemaphoreType.DMA((5,)),
            pltpu.SemaphoreType.DMA((3,)),
            pltpu.SemaphoreType.DMA((3, 3)),
            pltpu.SemaphoreType.DMA((3,)),
            pltpu.SemaphoreType.DMA((3,)),
            pltpu.SemaphoreType.DMA((3,)),
            pltpu.SemaphoreType.DMA((3,)),
            pltpu.SemaphoreType.DMA((3,)),
            pltpu.SemaphoreType.DMA((1,)),
            pltpu.SemaphoreType.DMA((5,)),
            pltpu.VMEM((F, E), BF),
            pltpu.VMEM((8, 3 * HD), F32),
            pltpu.VMEM((8, HD), F32),
            pltpu.SemaphoreType.DMA((4,)),
        ],
        compiler_params=pltpu.CompilerParams(
            collective_id=0, has_side_effects=True, vmem_limit_bytes=56 * 1024 * 1024
        ),
        cost_estimate=pl.CostEstimate(
            flops=2_000_000_000, bytes_accessed=4_000_000, transcendentals=400_000
        ),
    )(
        tables,
        jnp.transpose(sample_ids, (1, 2, 0)).reshape(16, NDP),
        table_slot.reshape(1, F),
        norm_gain.reshape(1, E),
        qkv_weight,
        out_weight,
        cotangent.reshape(F, E),
    )
    layer_out, pooled_grad, grad_qkv, grad_out = pl.pallas_call(
        finish,
        out_shape=(
            jax.ShapeDtypeStruct((F, E), BF),
            jax.ShapeDtypeStruct((NDP, 4, E), BF),
            jax.ShapeDtypeStruct((8, 3 * HD), F32),
            jax.ShapeDtypeStruct((8, HD), F32),
        ),
        in_specs=[vmem] * 4,
        out_specs=(vmem,) * 4,
        compiler_params=pltpu.CompilerParams(vmem_limit_bytes=56 * 1024 * 1024),
    )(*results)
    return (layer_out.reshape(1, F, E), pooled_grad, grad_qkv, grad_out)


def solution(mesh):
    return jax.shard_map(
        on_device,
        mesh=mesh,
        in_specs=(
            P("dp", None, None),
            P("rep", "dp", None),
            P(),
            P(),
            P("dp", None),
            P("dp", None),
            P(("rep", "dp"), None, None),
        ),
        out_specs=(
            P(("rep", "dp"), None, None),
            P("rep", "dp", None),
            P("dp", None),
            P("dp", None),
        ),
        check_vma=False,
    )
```

time: 82.3 us -> 73.9 us (0.90)
  local copies, waits for them, and re-layouts: 7.67 us -> 0 us
    unnamed x17 -> x0, local copies, waits for them, and re-layouts: 6.87 us -> none
    pallas_call x1, Pallas kernels: 73.6 us -> 71.1 us  [on_device(): pl.pallas_call(fused, out_shape=(jax.ShapeDtypeStruct((F, E), BF), jax.Sh...]
    pallas_call x0 -> x1, Pallas kernels: none -> 1.94 us  [on_device(): pl.pallas_call(finish, out_shape=(jax.ShapeDtypeStruct((F, E), BF), jax.S...]
where the time goes in v2:
time: 73.9 us; the launch traced here: 73.7 us
  Pallas kernels  73.1 us (99%)
    pallas_call x1, Pallas kernels, on_device(): pl.pallas_call(fused, out_shape=(jax.ShapeDtypeStruct((F, E), BF), jax.Sh...  71.1 us
    pallas_call x1, Pallas kernels, on_device(): pl.pallas_call(finish, out_shape=(jax.ShapeDtypeStruct((F, E), BF), jax.S...  1.94 us

profile of v2, /device:TPU:1, one launch (start us, length us, event | category | flops | bytes accessed | tf_op | source)
XLA Modules:
  0.0 73.7 jit_solution(15236253169938072801)
XLA Ops:
  0.6 71.1 %shard_map.102 = (bf16[256,512]{1,0:T(8,128)(2,1)}, bf16[64,16,128]{2,1,0:T(8,128)(2,1)}, f32[8,1152]{1,0:T(8,128)}, f32[8,384]{1,0:T(8,128)}) custom-call(bf16[4,256,512]{2,1,0:T(8,128)(2,1)} %tables_h.1, s32[16,64]{1,0:T(8,128)} %bitcast.9, s32[1,256]{1,0:T(1,128)} %bitcast.11, f32[1,512]{1,0:T(1,128)} %bitcast.10, bf16[8,1152]{1,0:T(8,128)(2,1)} %qkv.1, ...), custom_call_target="tpu_custom_call" | custom-call | flops 2000000000 | bytes 4000000 | tf_op jit(solution)/shard_map/pallas_call | solution.py:403
  71.8 1.9 %shard_map.103 = (bf16[256,512]{1,0:T(8,128)(2,1)}, bf16[64,4,512]{2,1,0:T(4,128)(2,1)}, f32[8,1152]{1,0:T(8,128)}, f32[8,384]{1,0:T(8,128)}) custom-call(bf16[256,512]{1,0:T(8,128)(2,1)} %get-tuple-element.12.layer_in, bf16[64,16,128]{2,1,0:T(8,128)(2,1)} %get-tuple-element.13.pooled_in, f32[8,1152]{1,0:T(8,128)} %get-tuple-element.14.qkv_in, ...), custom_call_target="tpu_custom_call" | custom-call | tf_op jit(solution)/shard_map/pallas_call | solution.py:467

commit v3 on v2

--- a/solution.py
+++ b/solution.py
@@ -52,8 +52,7 @@
     gt_recv,
     w_send,
     w_all,
-    wq,
-    wo,
+    wp,
     g_all,
     sib_recv,
     x_recv,
@@ -139,11 +138,12 @@
         load(i, src, dst)
 
     wide = jnp.concatenate([qkv[...].astype(F32), outw[...].astype(F32)], axis=1)
-    for k in range(6):
-        pair = jnp.concatenate(
-            [wide[:, 256 * k : 256 * k + 128], wide[:, 256 * k + 128 : 256 * k + 256]], axis=0
-        ).astype(BF)
-        w_send[k // 3, k % 3] = pair
+    for part in range(3):
+        for c in range(2):
+            first, second = 128 * (6 * c + part), 128 * (6 * c + part + 3)
+            w_send[c, part] = jnp.concatenate(
+                [wide[:, first : first + 128], wide[:, second : second + 128]], axis=0
+            ).astype(BF)
     for part in range(3):
         w_all[core, part, x, z * 2 + yh] = w_send[core, part]
 
@@ -203,50 +203,45 @@
             )
         to_sibling(part, x)
     forward(0)
-    forward(1)
+    loaded(2, *inputs[2])
+    loaded(3, *inputs[3])
+    loaded(4, *inputs[4])
+    slot_iota = lax.broadcasted_iota(jnp.int32, (F, F), 0)
+    place = jnp.where(slot_iota == slot[...], 1.0, 0.0).astype(BF)
+    cot_t = cot[...].T
 
     drain(tok_recv.at[pl.ds(0, NDP - 1)], recv_sem.at[1])
     rows_f[...] = tok_recv[...].reshape(NDP * 16, 128).astype(F32)
     by_slot = jnp.concatenate(
         [rows_f[pl.ds(cb, F, stride=4), :] for cb in range(4)], axis=1
     ).astype(BF)
-    loaded(2, *inputs[2])
-    loaded(3, *inputs[3])
-    slot_iota = lax.broadcasted_iota(jnp.int32, (F, F), 0)
-    place = jnp.where(slot_iota == slot[...], 1.0, 0.0).astype(BF)
     tokens = dot(place, by_slot, 0, 0)
     inv = lax.rsqrt(jnp.mean(tokens * tokens, axis=-1, keepdims=True) + EPS)
     normed = tokens * inv
     gains = gain[...]
     hidden = (normed * gains).astype(BF)
 
-    forward(2)
-    for part in range(3):
+    hidden_t = hidden.T
+
+    def whole(part):
         drain(w_all.at[other, part], ws_sem.at[part])
-        for k in (part, part + 3):
+        for c in range(2):
             for xx in range(NX):
-                both = w_all[k // 3, part, xx].astype(F32).reshape(NZ, 2, 2, 8, 128)
+                both = w_all[c, part, xx].astype(F32).reshape(NZ, 2, 2, 8, 128)
                 for half in range(2):
                     block = both[:, :, half].reshape(NZ, 16, 128).astype(BF)
-                    cb = 2 * k + half
+                    c0 = 256 * c + 128 * half
                     for zz in range(NZ):
                         r0 = 64 * zz + 16 * xx
-                        if cb < 9:
-                            wq[r0 : r0 + 16, 128 * cb : 128 * cb + 128] = block[zz]
-                        else:
-                            wo[r0 : r0 + 16, 128 * (cb - 9) : 128 * (cb - 9) + 128] = block[zz]
-
-    loaded(4, *inputs[4])
-    grad_context = dot(cot[...], wo[...], 1, 0).astype(BF)
-    projected = dot(hidden, wq[...], 1, 0).astype(BF)
+                        wp[part, r0 : r0 + 16, c0 : c0 + 128] = block[zz]
+
     low = lax.broadcasted_iota(jnp.int32, (F, 128), 1) < DH
     zero = jnp.zeros((F, 128), BF)
-    contexts, gq, gk, gv = [], [], [], []
-    for i in range(H // 2):
-        q2 = projected[:, 128 * i : 128 * i + 128]
-        k2 = projected[:, HD + 128 * i : HD + 128 * i + 128]
-        v2 = projected[:, 2 * HD + 128 * i : 2 * HD + 128 * i + 128]
-        c2 = grad_context[:, 128 * i : 128 * i + 128]
+
+    def attend(part):
+        projected = dot(hidden, wp[part, :, : 3 * 128], 1, 0).astype(BF)
+        q2, k2, v2 = projected[:, :128], projected[:, 128:256], projected[:, 256:]
+        c2 = dot(cot[...], wp[part, :, 3 * 128 :], 1, 0).astype(BF)
         parts = []
         for half in range(2):
             mine = low if half == 0 else jnp.logical_not(low)
@@ -259,49 +254,25 @@
             inner = jnp.sum(soft_f * grad_soft, axis=-1, keepdims=True)
             gs = (soft_f * (grad_soft - inner) * DH ** (-0.5)).astype(BF)
             parts.append((context, dot(gs, k2, 1, 0), dot(gs, q2, 0, 0), dot(soft, c2, 0, 0)))
-        for out, a, b in zip((contexts, gq, gk, gv), parts[0], parts[1]):
-            out.append(jnp.where(low, a, b).astype(BF))
-    context = jnp.concatenate(contexts, axis=1)
-    grad_projected = jnp.concatenate(gq + gk + gv, axis=1)
-
-    for part in range(3):
+        context, gq, gk, gv = (jnp.where(low, u, v).astype(BF) for u, v in zip(*parts))
+        return context, jnp.concatenate([gq, gk, gv], axis=1)
+
+    def terms(part, context, grad_projected):
+        heads = dot(hidden_t, grad_projected, 1, 0)
+        blocks = (
+            heads[:, :128],
+            heads[:, 128:256],
+            heads[:, 256:],
+            dot(cot_t, context, 1, 0),
+        )
+        blocks = [g.reshape(NZ, NX, 2, 8, 128) for g in blocks]
         for c in range(2):
-            k = 3 * c + part
-            blocks = []
-            for cb in (2 * k, 2 * k + 1):
-                if cb < 9:
-                    g = dot(hidden, grad_projected[:, 128 * cb : 128 * cb + 128], 0, 0)
-                else:
-                    g = dot(cot[...], context[:, 128 * (cb - 9) : 128 * (cb - 9) + 128], 0, 0)
-                blocks.append(g.reshape(NZ, NX, 2, 8, 128))
-            both = jnp.concatenate(blocks, axis=3).astype(BF)
+            both = jnp.concatenate(blocks[2 * c : 2 * c + 2], axis=3).astype(BF)
             for xx in range(NX):
                 g_all[c, part, xx] = both[:, xx].reshape(16, 16, 128)
         send(g_all.at[other, part], sib_recv.at[part], send_sem.at[4], sib_sem.at[part], sib)
 
-    scaled = dot(grad_projected, wq[...], 1, 1) * gains
-    grad_norm = inv * (scaled - normed * jnp.mean(scaled * normed, axis=-1, keepdims=True))
-    grad_tokens = (cot[...].astype(F32) + grad_norm).astype(BF)
-    turned = lax.rem(slot_iota, NDP) * 4 + slot_iota // NDP
-    place_back = jnp.where(turned == slot[...], 1.0, 0.0).astype(BF)
-    grad_slots = dot(place_back, grad_tokens, 1, 0)
-    for cb in range(4):
-        for j in range(4):
-            rows_f[pl.ds(4 * cb + j, NDP, stride=16), :] = grad_slots[
-                NDP * j : NDP * j + NDP, 128 * cb : 128 * cb + 128
-            ]
-    gt_send[...] = rows_f[...].astype(BF).reshape(NDP, 16, 128)
-
-    def send_grad(k, carry):
-        p = lax.rem(dp + k, NDP)
-        send(gt_send.at[p], gt_recv.at[dp], send_sem.at[6], recv_sem.at[4], (p, rep))
-        return carry
-
-    lax.fori_loop(1, NDP, send_grad, 0)
-    gt_recv[dp] = gt_send[dp]
-
-    mine = []
-    for part in range(3):
+    def over_x(part):
         drain(sib_recv.at[part], sib_sem.at[part])
         for k in range(NX):
             xx = lax.rem(x + 1 + k, NX)
@@ -315,9 +286,52 @@
                     x_sem.at[part],
                     (dp_of(z, xx, yh), rep),
                 )
-        mine.append(total)
-
-    layer_out[...] = (tokens + dot(context, wo[...], 1, 1)).astype(BF)
+        return total
+
+    forward(1)
+    whole(0)
+    context0, gp0 = attend(0)
+    terms(0, context0, gp0)
+    forward(2)
+    whole(1)
+    context1, gp1 = attend(1)
+    terms(1, context1, gp1)
+    mine = [over_x(0)]
+    whole(2)
+    context2, gp2 = attend(2)
+    terms(2, context2, gp2)
+    mine.append(over_x(1))
+
+    grad_hidden = dot(gp0, wp[0, :, : 3 * 128], 1, 1)
+    grad_hidden = grad_hidden + dot(gp1, wp[1, :, : 3 * 128], 1, 1)
+    grad_hidden = grad_hidden + dot(gp2, wp[2, :, : 3 * 128], 1, 1)
+    scaled = grad_hidden * gains
+    grad_norm = inv * (scaled - normed * jnp.mean(scaled * normed, axis=-1, keepdims=True))
+    grad_tokens = (cot[...].astype(F32) + grad_norm).astype(BF)
+    turned = lax.rem(slot_iota, NDP) * 4 + slot_iota // NDP
+    place_back = jnp.where(turned == slot[...], 1.0, 0.0).astype(BF)
+    grad_slots = dot(place_back, grad_tokens, 1, 0)
+    for cb in range(4):
+        for j in range(4):
+            rows_f[pl.ds(4 * cb + j, NDP, stride=16), :] = grad_slots[
+                NDP * j : NDP * j + NDP, 128 * cb : 128 * cb + 128
+            ]
+    gt_send[...] = rows_f[...].astype(BF).reshape(NDP, 16, 128)
+
+    def send_grad(k, carry):
+        p = lax.rem(dp + k, NDP)
+        send(gt_send.at[p], gt_recv.at[dp], send_sem.at[6], recv_sem.at[4], (p, rep))
+        return carry
+
+    lax.fori_loop(1, NDP, send_grad, 0)
+    gt_recv[dp] = gt_send[dp]
+
+    mine.append(over_x(2))
+
+    branch = dot(context0, wp[0, :, 3 * 128 :], 1, 1)
+    branch = branch + dot(context1, wp[1, :, 3 * 128 :], 1, 1)
+    branch = branch + dot(context2, wp[2, :, 3 * 128 :], 1, 1)
+    layer_out[...] = (tokens + branch).astype(BF)
     outputs = (
         (layer_out, layer_out_h),
         (gt_recv, pooled_grad_h),
@@ -367,7 +381,8 @@
 
     drain(fin.at[other], fin_sem.at[0])
     for cb in range(12):
-        piece = fin[cb // 6, (cb % 6) // 2, 8 * (cb % 2) : 8 * (cb % 2) + 8, :]
+        half = 8 * (cb % 6 // 3)
+        piece = fin[cb // 6, cb % 3, half : half + 8, :]
         if cb < 9:
             grad_qkv[:, 128 * cb : 128 * cb + 128] = piece
         else:
@@ -423,8 +438,7 @@
             pltpu.VMEM((NDP, 16, 128), BF),
             pltpu.VMEM((2, 3, 16, 128), BF),
             pltpu.VMEM((2, 3, NX, 16, 16, 128), BF),
-            pltpu.VMEM((E, 3 * HD), BF),
-            pltpu.VMEM((E, HD), BF),
+            pltpu.VMEM((3, E, 4 * 128), BF),
             pltpu.VMEM((2, 3, NX, 16, 16, 128), BF),
             pltpu.VMEM((3, NX, 16, 16, 128), BF),
             pltpu.VMEM((3, NX - 1, 16, 16, 128), BF),

time: 73.9 us -> 68.5 us (0.927)
  Pallas kernels: 73.1 us -> 67.7 us
    pallas_call x1, Pallas kernels: 71.1 us -> 65.7 us  [on_device(): pl.pallas_call(fused, out_shape=(jax.ShapeDtypeStruct((F, E), BF), jax.Sh...]
where the time goes in v3:
time: 68.5 us; the launch traced here: 68.3 us
  Pallas kernels  67.7 us (99%)
    pallas_call x1, Pallas kernels, on_device(): pl.pallas_call(fused, out_shape=(jax.ShapeDtypeStruct((F, E), BF), jax.Sh...  65.7 us
    pallas_call x1, Pallas kernels, on_device(): pl.pallas_call(finish, out_shape=(jax.ShapeDtypeStruct((F, E), BF), jax.S...  1.94 us

profile of v3, /device:TPU:1, one launch (start us, length us, event | category | flops | bytes accessed | tf_op | source)
XLA Modules:
  0.0 68.3 jit_solution(3313601580024252399)
XLA Ops:
  0.6 65.7 %shard_map.102 = (bf16[256,512]{1,0:T(8,128)(2,1)}, bf16[64,16,128]{2,1,0:T(8,128)(2,1)}, f32[8,1152]{1,0:T(8,128)}, f32[8,384]{1,0:T(8,128)}) custom-call(bf16[4,256,512]{2,1,0:T(8,128)(2,1)} %tables_h.1, s32[16,64]{1,0:T(8,128)} %bitcast.9, s32[1,256]{1,0:T(1,128)} %bitcast.11, f32[1,512]{1,0:T(1,128)} %bitcast.10, bf16[8,1152]{1,0:T(8,128)(2,1)} %qkv.1, ...), custom_call_target="tpu_custom_call" | custom-call | flops 2000000000 | bytes 4000000 | tf_op jit(solution)/shard_map/pallas_call | solution.py:418
  66.4 1.9 %shard_map.103 = (bf16[256,512]{1,0:T(8,128)(2,1)}, bf16[64,4,512]{2,1,0:T(4,128)(2,1)}, f32[8,1152]{1,0:T(8,128)}, f32[8,384]{1,0:T(8,128)}) custom-call(bf16[256,512]{1,0:T(8,128)(2,1)} %get-tuple-element.12.layer_in, bf16[64,16,128]{2,1,0:T(8,128)(2,1)} %get-tuple-element.13.pooled_in, f32[8,1152]{1,0:T(8,128)} %get-tuple-element.14.qkv_in, ...), custom_call_target="tpu_custom_call" | custom-call | tf_op jit(solution)/shard_map/pallas_call | solution.py:481

commit v4 on v3

--- a/solution.py
+++ b/solution.py
@@ -302,6 +302,22 @@
     terms(2, context2, gp2)
     mine.append(over_x(1))
 
+    def over_z(part):
+        drain(x_recv.at[part], x_sem.at[part])
+        total = mine[part]
+        for k in range(NX - 1):
+            total = total + x_recv[part, k].astype(F32)
+        s2[part] = total.astype(BF).reshape(NZ, 2, 16, 128)
+        for k in range(1, NZ):
+            zz = lax.rem(z + k, NZ)
+            send(
+                s2.at[part, zz],
+                z_recv.at[part, k - 1],
+                send_sem.at[7],
+                z_sem.at[part],
+                (dp_of(zz, x, yh), rep),
+            )
+
     grad_hidden = dot(gp0, wp[0, :, : 3 * 128], 1, 1)
     grad_hidden = grad_hidden + dot(gp1, wp[1, :, : 3 * 128], 1, 1)
     grad_hidden = grad_hidden + dot(gp2, wp[2, :, : 3 * 128], 1, 1)
@@ -318,6 +334,9 @@
             ]
     gt_send[...] = rows_f[...].astype(BF).reshape(NDP, 16, 128)
 
+    mine.append(over_x(2))
+    over_z(0)
+
     def send_grad(k, carry):
         p = lax.rem(dp + k, NDP)
         send(gt_send.at[p], gt_recv.at[dp], send_sem.at[6], recv_sem.at[4], (p, rep))
@@ -326,8 +345,7 @@
     lax.fori_loop(1, NDP, send_grad, 0)
     gt_recv[dp] = gt_send[dp]
 
-    mine.append(over_x(2))
-
+    over_z(1)
     branch = dot(context0, wp[0, :, 3 * 128 :], 1, 1)
     branch = branch + dot(context1, wp[1, :, 3 * 128 :], 1, 1)
     branch = branch + dot(context2, wp[2, :, 3 * 128 :], 1, 1)
@@ -343,22 +361,7 @@
         return pltpu.make_async_copy(*outputs[i], out_sem.at[i])
 
     store(0).start()
-
-    for part in range(3):
-        drain(x_recv.at[part], x_sem.at[part])
-        total = mine[part]
-        for k in range(NX - 1):
-            total = total + x_recv[part, k].astype(F32)
-        s2[part] = total.astype(BF).reshape(NZ, 2, 16, 128)
-        for k in range(1, NZ):
-            zz = lax.rem(z + k, NZ)
-            send(
-                s2.at[part, zz],
-                z_recv.at[part, k - 1],
-                send_sem.at[7],
-                z_sem.at[part],
-                (dp_of(zz, x, yh), rep),
-            )
+    over_z(2)
 
     for part in range(3):
         total = s2[part, z].astype(F32)

time: 68.5 us -> 67.9 us (level)
  Pallas kernels: 67.7 us -> 67 us
where the time goes in v4:
time: 67.9 us; the launch traced here: 67.7 us
  Pallas kernels  67 us (99%)
    pallas_call x1, Pallas kernels, on_device(): pl.pallas_call(fused, out_shape=(jax.ShapeDtypeStruct((F, E), BF), jax.Sh...  65.1 us
    pallas_call x1, Pallas kernels, on_device(): pl.pallas_call(finish, out_shape=(jax.ShapeDtypeStruct((F, E), BF), jax.S...  1.94 us

profile of v4, /device:TPU:1, one launch (start us, length us, event | category | flops | bytes accessed | tf_op | source)
XLA Modules:
  0.0 67.7 jit_solution(15173315623194334456)
XLA Ops:
  0.6 65.1 %shard_map.102 = (bf16[256,512]{1,0:T(8,128)(2,1)}, bf16[64,16,128]{2,1,0:T(8,128)(2,1)}, f32[8,1152]{1,0:T(8,128)}, f32[8,384]{1,0:T(8,128)}) custom-call(bf16[4,256,512]{2,1,0:T(8,128)(2,1)} %tables_h.1, s32[16,64]{1,0:T(8,128)} %bitcast.9, s32[1,256]{1,0:T(1,128)} %bitcast.11, f32[1,512]{1,0:T(1,128)} %bitcast.10, bf16[8,1152]{1,0:T(8,128)(2,1)} %qkv.1, ...), custom_call_target="tpu_custom_call" | custom-call | flops 2000000000 | bytes 4000000 | tf_op jit(solution)/shard_map/pallas_call | solution.py:421
  65.7 1.9 %shard_map.103 = (bf16[256,512]{1,0:T(8,128)(2,1)}, bf16[64,4,512]{2,1,0:T(4,128)(2,1)}, f32[8,1152]{1,0:T(8,128)}, f32[8,384]{1,0:T(8,128)}) custom-call(bf16[256,512]{1,0:T(8,128)(2,1)} %get-tuple-element.12.layer_in, bf16[64,16,128]{2,1,0:T(8,128)(2,1)} %get-tuple-element.13.pooled_in, f32[8,1152]{1,0:T(8,128)} %get-tuple-element.14.qkv_in, ...), custom_call_target="tpu_custom_call" | custom-call | tf_op jit(solution)/shard_map/pallas_call | solution.py:484
